TPU v7x, 512 devices: a whole 4x8x8 slice. The times are simulated.
512 devices in a mesh: store: 32 (over z, y_lo, core), prod: 16 (over y_hi, x).
Axes of the slice: x: 4, y: 8 (y_hi: 4, y_lo: 2; y = y_hi * 2 + y_lo), z: 8, core: 2. Of those that a mesh axis runs over, the one named last changes fastest.
Arguments:
- gradients: bfloat16 [196608, 2048], P(('store', 'prod')), may hold values from -6 to 6
- destinations: int32 [196608], P(('store', 'prod')), may hold values from 0 to 31, as said below
- queries: bfloat16 [1536, 2048], P(('store', 'prod')), may hold values from -6 to 6
- left_factor: float32 [32, 32], replicated, may hold values from -11 to 11, as said below
- right_factor: float32 [64, 64], replicated, may hold values from -11 to 11, as said below
Outputs:
- scores: bfloat16 [1536, 393216], P(None, ('store', 'prod'))
Inputs may be any that keep to these rules, and one draw needn't show every extreme that they name: `destinations`: within the rows of one producer (aligned blocks of 384 rows) no store index is named more than 24 times, and one store index, the same for every producer, is named exactly 24 times in every block. `left_factor`: a dense real matrix. `right_factor`: a dense real matrix.
All inputs are finite; a program needn't handle non-finite values.
Results may differ from a plain program's by a relative error of at most 0.0049.
Values may be sent and summed in bfloat16 or wider, within the bound.
No kernel may reach another device: no remote copies, remote signals or barrier semaphores. Data moves between devices by JAX's collectives and lax.ppermute only.
A program may use at most 64 MiB of HBM per device.

v0:
```python
import math
import jax
import jax.numpy as jnp
from jax import lax
from jax.sharding import PartitionSpec as P


def from_behind(block, axis, distance):
    devices = range(lax.axis_size(axis))
    route = [((i - distance) % len(devices), i) for i in devices]
    return lax.ppermute(block, axis, route)


def precondition(gradients, left_factor, right_factor):
    left_size = left_factor.shape[0]
    right_size = right_factor.shape[0]
    leading = gradients.shape[:-1]
    matrices = gradients.astype(jnp.float32).reshape((-1, left_size, right_size))
    right_done = jnp.einsum("nbc,cd->nbd", matrices, right_factor, precision=lax.Precision.HIGHEST)
    product = jnp.einsum("ab,nbd->nad", left_factor, right_done, precision=lax.Precision.HIGHEST)
    product = product.reshape(leading + (left_size * right_size,))
    scaling = lax.rsqrt(jnp.mean(product * product, axis=-1, keepdims=True) + 1e-06)
    return (product * scaling * (1.0 / math.sqrt(left_size * right_size))).astype(jnp.bfloat16)


def row_ranks(targets, owners):
    matches = (targets[:, None] == jnp.arange(owners, dtype=jnp.int32)[None, :]).astype(jnp.int32)
    earlier = jnp.cumsum(matches, axis=0) - matches
    return jnp.sum(earlier * matches, axis=1)


def fill_tile(scores, local_block, position, stored):
    product = lax.dot_general(
        local_block, stored, (((1,), (1,)), ((), ())), preferred_element_type=jnp.float32
    )
    return lax.dynamic_update_slice_in_dim(
        scores, product.astype(jnp.bfloat16), position * local_block.shape[0], 0
    )


def body(gradients, destinations, queries, left_factor, right_factor):
    owners = lax.axis_size("store")
    own_index = lax.axis_index("store")
    row_count, feature_width = gradients.shape
    bucket = 2 * row_count // owners
    capacity = owners * bucket
    places = destinations * bucket + row_ranks(destinations, owners)
    local_queries = lax.all_gather(queries, "prod", axis=0, tiled=True)
    blank_scores = jnp.zeros((local_queries.shape[0] * owners, capacity), jnp.bfloat16)
    buffer = jnp.zeros((capacity, feature_width), jnp.bfloat16).at[places].set(gradients)
    buffer = buffer.reshape((owners, bucket, feature_width))
    stored = precondition(
        lax.all_to_all(buffer, "store", split_axis=0, concat_axis=0, tiled=True),
        left_factor,
        right_factor,
    ).reshape((capacity, feature_width))
    scores = fill_tile(blank_scores, local_queries, own_index, stored)

    def advance(turn_index, cycle_state):
        current, moving = cycle_state
        moving = from_behind(moving, "store", 1)
        current = fill_tile(current, moving, (own_index - turn_index) % owners, stored)
        return (current, moving)

    scores, moving = lax.fori_loop(1, owners, advance, (scores, local_queries))
    return scores


def solution(mesh):
    return jax.shard_map(
        body,
        mesh=mesh,
        in_specs=(
            P(("store", "prod"), None),
            P(("store", "prod")),
            P(("store", "prod"), None),
            P(),
            P(),
        ),
        out_specs=P(None, ("store", "prod")),
        check_vma=False,
    )
```

profile of v0, /device:TPU:258, one launch (start us, length us, event | category | flops | bytes accessed | tf_op | source)
XLA Modules:
  0.0 516.4 jit_solution(16796309453098849389)
XLA Ops:
  9.2 8.5 %all-to-all-start = ((bf16[32,24,2048]{2,1,0:T(8,128)(2,1)}), bf16[32,24,2048]{2,1,0:T(8,128)(2,1)S(1)}, u32[]{:S(2)}, u32[]{:S(2)}) async-start(bf16[32,24,2048]{2,1,0:T(8,128)(2,1)} %bitcast.2), calls=%async_computation | async-start | bytes 6291456 | tf_op jit(solution)/shard_map/all_to_all | solution.py:53
  17.7 95.6 %all-gather = bf16[16,3,2048]{2,1,0:T(4,128)(2,1)S(1)} all-gather(bf16[1,3,2048]{2,1,0:T(4,128)(2,1)S(1)} %bitcast.52), channel_id=1, replica_groups=mesh['store'=32,'prod'=16] {'prod'}, dimensions={0}, use_global_device_ids=true | all-gather | bytes 208896 | tf_op jit(solution)/shard_map/all_gather | solution.py:48
  114.2 7.6 %reshape.42 = bf16[768,32,64]{2,1,0:T(8,128)(2,1)} reshape(bf16[32,24,2048]{2,1,0:T(8,128)(2,1)S(1)} %all-to-all-done) | data formatting | bytes 6291456 | tf_op jit(solution)/shard_map/reshape | solution.py:18
  121.9 9.0 %fusion.5 = f32[768,32,64]{0,2,1:T(8,128)S(1)} fusion(bf16[768,32,64]{2,1,0:T(8,128)(2,1)} %reshape.42, f32[64,64]{1,0:T(8,128)S(1)} %copy-done), kind=kOutput, calls=%fused_computation.8 | convolution fusion | flops 1207959552 | bytes 9453568 | tf_op jit(solution)/shard_map/nbc,cd->nbd/dot_general | solution.py:19
  130.9 10.1 %multiply_reduce_fusion = (f32[768]{0:T(1024)S(1)}, f32[768,32,64]{0,1,2:T(8,128)S(1)}) fusion(f32[32,32]{1,0:T(8,128)S(1)} %copy-done.2, f32[768,32,64]{0,2,1:T(8,128)S(1)} %fusion.5), kind=kOutput, calls=%fused_computation.10 | convolution fusion | flops 607124736 | bytes 12590080 | tf_op jit(solution)/shard_map/ab,nbd->nad/dot_general | solution.py:20
  154.7 361.7 %while.17 = (s32[]{:T(128)}, bf16[1536,768]{1,0:T(8,128)(2,1)}, bf16[48,2048]{1,0:T(8,128)(2,1)}, bf16[768,2048]{1,0:T(8,128)(2,1)S(1)}, s32[]{:T(128)}, /*index...) while((s32[]{:T(128)}, bf16[1536,768]{1,0:T(8,128)(2,1)}, ...), condition=%wide.region_6.7_spmd, body=%wide.region_5.6_spmd.sunk | while | flops 151031824 | bytes 4596032 | solution.py:65
  156.7 7.4 %collective-permute-done = bf16[48,2048]{1,0:T(8,128)(2,1)S(1)} collective-permute-done((bf16[48,2048]{1,0:T(8,128)(2,1)}, bf16[48,2048]{1,0:T(8,128)(2,1)S(1)}, u32[]{:S(2)}, u32[]{:S(2)}) %collective-permute-start) | collective-permute-done | bytes 196640 | tf_op jit(solution)/shard_map/while/body/eval_jaxpr/ppermute | solution.py:11
  168.3 7.4 %collective-permute-done = bf16[48,2048]{1,0:T(8,128)(2,1)S(1)} collective-permute-done((bf16[48,2048]{1,0:T(8,128)(2,1)}, bf16[48,2048]{1,0:T(8,128)(2,1)S(1)}, u32[]{:S(2)}, u32[]{:S(2)}) %collective-permute-start) | collective-permute-done | bytes 196640 | tf_op jit(solution)/shard_map/while/body/eval_jaxpr/ppermute | solution.py:11
  191.7 7.4 %collective-permute-done = bf16[48,2048]{1,0:T(8,128)(2,1)S(1)} collective-permute-done((bf16[48,2048]{1,0:T(8,128)(2,1)}, bf16[48,2048]{1,0:T(8,128)(2,1)S(1)}, u32[]{:S(2)}, u32[]{:S(2)}) %collective-permute-start) | collective-permute-done | bytes 196640 | tf_op jit(solution)/shard_map/while/body/eval_jaxpr/ppermute | solution.py:11
  203.3 7.4 %collective-permute-done = bf16[48,2048]{1,0:T(8,128)(2,1)S(1)} collective-permute-done((bf16[48,2048]{1,0:T(8,128)(2,1)}, bf16[48,2048]{1,0:T(8,128)(2,1)S(1)}, u32[]{:S(2)}, u32[]{:S(2)}) %collective-permute-start) | collective-permute-done | bytes 196640 | tf_op jit(solution)/shard_map/while/body/eval_jaxpr/ppermute | solution.py:11
  226.7 7.4 %collective-permute-done = bf16[48,2048]{1,0:T(8,128)(2,1)S(1)} collective-permute-done((bf16[48,2048]{1,0:T(8,128)(2,1)}, bf16[48,2048]{1,0:T(8,128)(2,1)S(1)}, u32[]{:S(2)}, u32[]{:S(2)}) %collective-permute-start) | collective-permute-done | bytes 196640 | tf_op jit(solution)/shard_map/while/body/eval_jaxpr/ppermute | solution.py:11
  238.3 7.4 %collective-permute-done = bf16[48,2048]{1,0:T(8,128)(2,1)S(1)} collective-permute-done((bf16[48,2048]{1,0:T(8,128)(2,1)}, bf16[48,2048]{1,0:T(8,128)(2,1)S(1)}, u32[]{:S(2)}, u32[]{:S(2)}) %collective-permute-start) | collective-permute-done | bytes 196640 | tf_op jit(solution)/shard_map/while/body/eval_jaxpr/ppermute | solution.py:11
  250.0 7.4 %collective-permute-done = bf16[48,2048]{1,0:T(8,128)(2,1)S(1)} collective-permute-done((bf16[48,2048]{1,0:T(8,128)(2,1)}, bf16[48,2048]{1,0:T(8,128)(2,1)S(1)}, u32[]{:S(2)}, u32[]{:S(2)}) %collective-permute-start) | collective-permute-done | bytes 196640 | tf_op jit(solution)/shard_map/while/body/eval_jaxpr/ppermute | solution.py:11
  261.7 7.4 %collective-permute-done = bf16[48,2048]{1,0:T(8,128)(2,1)S(1)} collective-permute-done((bf16[48,2048]{1,0:T(8,128)(2,1)}, bf16[48,2048]{1,0:T(8,128)(2,1)S(1)}, u32[]{:S(2)}, u32[]{:S(2)}) %collective-permute-start) | collective-permute-done | bytes 196640 | tf_op jit(solution)/shard_map/while/body/eval_jaxpr/ppermute | solution.py:11
  273.3 7.4 %collective-permute-done = bf16[48,2048]{1,0:T(8,128)(2,1)S(1)} collective-permute-done((bf16[48,2048]{1,0:T(8,128)(2,1)}, bf16[48,2048]{1,0:T(8,128)(2,1)S(1)}, u32[]{:S(2)}, u32[]{:S(2)}) %collective-permute-start) | collective-permute-done | bytes 196640 | tf_op jit(solution)/shard_map/while/body/eval_jaxpr/ppermute | solution.py:11
  285.0 7.4 %collective-permute-done = bf16[48,2048]{1,0:T(8,128)(2,1)S(1)} collective-permute-done((bf16[48,2048]{1,0:T(8,128)(2,1)}, bf16[48,2048]{1,0:T(8,128)(2,1)S(1)}, u32[]{:S(2)}, u32[]{:S(2)}) %collective-permute-start) | collective-permute-done | bytes 196640 | tf_op jit(solution)/shard_map/while/body/eval_jaxpr/ppermute | solution.py:11
  296.7 7.4 %collective-permute-done = bf16[48,2048]{1,0:T(8,128)(2,1)S(1)} collective-permute-done((bf16[48,2048]{1,0:T(8,128)(2,1)}, bf16[48,2048]{1,0:T(8,128)(2,1)S(1)}, u32[]{:S(2)}, u32[]{:S(2)}) %collective-permute-start) | collective-permute-done | bytes 196640 | tf_op jit(solution)/shard_map/while/body/eval_jaxpr/ppermute | solution.py:11
  308.3 7.4 %collective-permute-done = bf16[48,2048]{1,0:T(8,128)(2,1)S(1)} collective-permute-done((bf16[48,2048]{1,0:T(8,128)(2,1)}, bf16[48,2048]{1,0:T(8,128)(2,1)S(1)}, u32[]{:S(2)}, u32[]{:S(2)}) %collective-permute-start) | collective-permute-done | bytes 196640 | tf_op jit(solution)/shard_map/while/body/eval_jaxpr/ppermute | solution.py:11
  331.7 7.4 %collective-permute-done = bf16[48,2048]{1,0:T(8,128)(2,1)S(1)} collective-permute-done((bf16[48,2048]{1,0:T(8,128)(2,1)}, bf16[48,2048]{1,0:T(8,128)(2,1)S(1)}, u32[]{:S(2)}, u32[]{:S(2)}) %collective-permute-start) | collective-permute-done | bytes 196640 | tf_op jit(solution)/shard_map/while/body/eval_jaxpr/ppermute | solution.py:11
  355.0 7.4 %collective-permute-done = bf16[48,2048]{1,0:T(8,128)(2,1)S(1)} collective-permute-done((bf16[48,2048]{1,0:T(8,128)(2,1)}, bf16[48,2048]{1,0:T(8,128)(2,1)S(1)}, u32[]{:S(2)}, u32[]{:S(2)}) %collective-permute-start) | collective-permute-done | bytes 196640 | tf_op jit(solution)/shard_map/while/body/eval_jaxpr/ppermute | solution.py:11
  366.7 7.4 %collective-permute-done = bf16[48,2048]{1,0:T(8,128)(2,1)S(1)} collective-permute-done((bf16[48,2048]{1,0:T(8,128)(2,1)}, bf16[48,2048]{1,0:T(8,128)(2,1)S(1)}, u32[]{:S(2)}, u32[]{:S(2)}) %collective-permute-start) | collective-permute-done | bytes 196640 | tf_op jit(solution)/shard_map/while/body/eval_jaxpr/ppermute | solution.py:11
  378.3 7.4 %collective-permute-done = bf16[48,2048]{1,0:T(8,128)(2,1)S(1)} collective-permute-done((bf16[48,2048]{1,0:T(8,128)(2,1)}, bf16[48,2048]{1,0:T(8,128)(2,1)S(1)}, u32[]{:S(2)}, u32[]{:S(2)}) %collective-permute-start) | collective-permute-done | bytes 196640 | tf_op jit(solution)/shard_map/while/body/eval_jaxpr/ppermute | solution.py:11
  390.0 7.4 %collective-permute-done = bf16[48,2048]{1,0:T(8,128)(2,1)S(1)} collective-permute-done((bf16[48,2048]{1,0:T(8,128)(2,1)}, bf16[48,2048]{1,0:T(8,128)(2,1)S(1)}, u32[]{:S(2)}, u32[]{:S(2)}) %collective-permute-start) | collective-permute-done | bytes 196640 | tf_op jit(solution)/shard_map/while/body/eval_jaxpr/ppermute | solution.py:11
  401.7 7.4 %collective-permute-done = bf16[48,2048]{1,0:T(8,128)(2,1)S(1)} collective-permute-done((bf16[48,2048]{1,0:T(8,128)(2,1)}, bf16[48,2048]{1,0:T(8,128)(2,1)S(1)}, u32[]{:S(2)}, u32[]{:S(2)}) %collective-permute-start) | collective-permute-done | bytes 196640 | tf_op jit(solution)/shard_map/while/body/eval_jaxpr/ppermute | solution.py:11
  (129 shorter events, 251.8 us)
Async XLA Ops:
  9.2 105.1 %all-to-all-start = ((bf16[32,24,2048]{2,1,0:T(8,128)(2,1)}), bf16[32,24,2048]{2,1,0:T(8,128)(2,1)S(1)}, u32[]{:S(2)}, u32[]{:S(2)}) async-start(bf16[32,24,2048]{2,1,0:T(8,128)(2,1)} %bitcast.2), calls=%async_computation | async-start | bytes 6291456 | tf_op jit(solution)/shard_map/all_to_all | solution.py:53
  154.7 9.3 %collective-permute-start = (bf16[48,2048]{1,0:T(8,128)(2,1)}, bf16[48,2048]{1,0:T(8,128)(2,1)S(1)}, u32[]{:S(2)}, u32[]{:S(2)}) collective-permute-start(bf16[48,2048]{1,0:T(8,128)(2,1)} %get-tuple-element.205), channel_id=1, source_target_pairs={{496,0},{0,16},{16,32},{32,48},{48,64},{64,80},{80,96},{96,112},{1... | collective-permute-start | bytes 589832 | tf_op jit(solution)/shard_map/while/body/eval_jaxpr/ppermute | solution.py:11
  166.4 9.3 %collective-permute-start = (bf16[48,2048]{1,0:T(8,128)(2,1)}, bf16[48,2048]{1,0:T(8,128)(2,1)S(1)}, u32[]{:S(2)}, u32[]{:S(2)}) collective-permute-start(bf16[48,2048]{1,0:T(8,128)(2,1)} %get-tuple-element.205), channel_id=1, source_target_pairs={{496,0},{0,16},{16,32},{32,48},{48,64},{64,80},{80,96},{96,112},{1... | collective-permute-start | bytes 589832 | tf_op jit(solution)/shard_map/while/body/eval_jaxpr/ppermute | solution.py:11
  189.7 9.3 %collective-permute-start = (bf16[48,2048]{1,0:T(8,128)(2,1)}, bf16[48,2048]{1,0:T(8,128)(2,1)S(1)}, u32[]{:S(2)}, u32[]{:S(2)}) collective-permute-start(bf16[48,2048]{1,0:T(8,128)(2,1)} %get-tuple-element.205), channel_id=1, source_target_pairs={{496,0},{0,16},{16,32},{32,48},{48,64},{64,80},{80,96},{96,112},{1... | collective-permute-start | bytes 589832 | tf_op jit(solution)/shard_map/while/body/eval_jaxpr/ppermute | solution.py:11
  224.7 9.3 %collective-permute-start = (bf16[48,2048]{1,0:T(8,128)(2,1)}, bf16[48,2048]{1,0:T(8,128)(2,1)S(1)}, u32[]{:S(2)}, u32[]{:S(2)}) collective-permute-start(bf16[48,2048]{1,0:T(8,128)(2,1)} %get-tuple-element.205), channel_id=1, source_target_pairs={{496,0},{0,16},{16,32},{32,48},{48,64},{64,80},{80,96},{96,112},{1... | collective-permute-start | bytes 589832 | tf_op jit(solution)/shard_map/while/body/eval_jaxpr/ppermute | solution.py:11
  236.4 9.3 %collective-permute-start = (bf16[48,2048]{1,0:T(8,128)(2,1)}, bf16[48,2048]{1,0:T(8,128)(2,1)S(1)}, u32[]{:S(2)}, u32[]{:S(2)}) collective-permute-start(bf16[48,2048]{1,0:T(8,128)(2,1)} %get-tuple-element.205), channel_id=1, source_target_pairs={{496,0},{0,16},{16,32},{32,48},{48,64},{64,80},{80,96},{96,112},{1... | collective-permute-start | bytes 589832 | tf_op jit(solution)/shard_map/while/body/eval_jaxpr/ppermute | solution.py:11
  248.1 9.3 %collective-permute-start = (bf16[48,2048]{1,0:T(8,128)(2,1)}, bf16[48,2048]{1,0:T(8,128)(2,1)S(1)}, u32[]{:S(2)}, u32[]{:S(2)}) collective-permute-start(bf16[48,2048]{1,0:T(8,128)(2,1)} %get-tuple-element.205), channel_id=1, source_target_pairs={{496,0},{0,16},{16,32},{32,48},{48,64},{64,80},{80,96},{96,112},{1... | collective-permute-start | bytes 589832 | tf_op jit(solution)/shard_map/while/body/eval_jaxpr/ppermute | solution.py:11
  259.7 9.3 %collective-permute-start = (bf16[48,2048]{1,0:T(8,128)(2,1)}, bf16[48,2048]{1,0:T(8,128)(2,1)S(1)}, u32[]{:S(2)}, u32[]{:S(2)}) collective-permute-start(bf16[48,2048]{1,0:T(8,128)(2,1)} %get-tuple-element.205), channel_id=1, source_target_pairs={{496,0},{0,16},{16,32},{32,48},{48,64},{64,80},{80,96},{96,112},{1... | collective-permute-start | bytes 589832 | tf_op jit(solution)/shard_map/while/body/eval_jaxpr/ppermute | solution.py:11
  271.4 9.3 %collective-permute-start = (bf16[48,2048]{1,0:T(8,128)(2,1)}, bf16[48,2048]{1,0:T(8,128)(2,1)S(1)}, u32[]{:S(2)}, u32[]{:S(2)}) collective-permute-start(bf16[48,2048]{1,0:T(8,128)(2,1)} %get-tuple-element.205), channel_id=1, source_target_pairs={{496,0},{0,16},{16,32},{32,48},{48,64},{64,80},{80,96},{96,112},{1... | collective-permute-start | bytes 589832 | tf_op jit(solution)/shard_map/while/body/eval_jaxpr/ppermute | solution.py:11
  283.1 9.3 %collective-permute-start = (bf16[48,2048]{1,0:T(8,128)(2,1)}, bf16[48,2048]{1,0:T(8,128)(2,1)S(1)}, u32[]{:S(2)}, u32[]{:S(2)}) collective-permute-start(bf16[48,2048]{1,0:T(8,128)(2,1)} %get-tuple-element.205), channel_id=1, source_target_pairs={{496,0},{0,16},{16,32},{32,48},{48,64},{64,80},{80,96},{96,112},{1... | collective-permute-start | bytes 589832 | tf_op jit(solution)/shard_map/while/body/eval_jaxpr/ppermute | solution.py:11
  294.7 9.3 %collective-permute-start = (bf16[48,2048]{1,0:T(8,128)(2,1)}, bf16[48,2048]{1,0:T(8,128)(2,1)S(1)}, u32[]{:S(2)}, u32[]{:S(2)}) collective-permute-start(bf16[48,2048]{1,0:T(8,128)(2,1)} %get-tuple-element.205), channel_id=1, source_target_pairs={{496,0},{0,16},{16,32},{32,48},{48,64},{64,80},{80,96},{96,112},{1... | collective-permute-start | bytes 589832 | tf_op jit(solution)/shard_map/while/body/eval_jaxpr/ppermute | solution.py:11
  306.4 9.3 %collective-permute-start = (bf16[48,2048]{1,0:T(8,128)(2,1)}, bf16[48,2048]{1,0:T(8,128)(2,1)S(1)}, u32[]{:S(2)}, u32[]{:S(2)}) collective-permute-start(bf16[48,2048]{1,0:T(8,128)(2,1)} %get-tuple-element.205), channel_id=1, source_target_pairs={{496,0},{0,16},{16,32},{32,48},{48,64},{64,80},{80,96},{96,112},{1... | collective-permute-start | bytes 589832 | tf_op jit(solution)/shard_map/while/body/eval_jaxpr/ppermute | solution.py:11
  329.7 9.3 %collective-permute-start = (bf16[48,2048]{1,0:T(8,128)(2,1)}, bf16[48,2048]{1,0:T(8,128)(2,1)S(1)}, u32[]{:S(2)}, u32[]{:S(2)}) collective-permute-start(bf16[48,2048]{1,0:T(8,128)(2,1)} %get-tuple-element.205), channel_id=1, source_target_pairs={{496,0},{0,16},{16,32},{32,48},{48,64},{64,80},{80,96},{96,112},{1... | collective-permute-start | bytes 589832 | tf_op jit(solution)/shard_map/while/body/eval_jaxpr/ppermute | solution.py:11
  353.1 9.3 %collective-permute-start = (bf16[48,2048]{1,0:T(8,128)(2,1)}, bf16[48,2048]{1,0:T(8,128)(2,1)S(1)}, u32[]{:S(2)}, u32[]{:S(2)}) collective-permute-start(bf16[48,2048]{1,0:T(8,128)(2,1)} %get-tuple-element.205), channel_id=1, source_target_pairs={{496,0},{0,16},{16,32},{32,48},{48,64},{64,80},{80,96},{96,112},{1... | collective-permute-start | bytes 589832 | tf_op jit(solution)/shard_map/while/body/eval_jaxpr/ppermute | solution.py:11
  364.7 9.3 %collective-permute-start = (bf16[48,2048]{1,0:T(8,128)(2,1)}, bf16[48,2048]{1,0:T(8,128)(2,1)S(1)}, u32[]{:S(2)}, u32[]{:S(2)}) collective-permute-start(bf16[48,2048]{1,0:T(8,128)(2,1)} %get-tuple-element.205), channel_id=1, source_target_pairs={{496,0},{0,16},{16,32},{32,48},{48,64},{64,80},{80,96},{96,112},{1... | collective-permute-start | bytes 589832 | tf_op jit(solution)/shard_map/while/body/eval_jaxpr/ppermute | solution.py:11
  376.4 9.3 %collective-permute-start = (bf16[48,2048]{1,0:T(8,128)(2,1)}, bf16[48,2048]{1,0:T(8,128)(2,1)S(1)}, u32[]{:S(2)}, u32[]{:S(2)}) collective-permute-start(bf16[48,2048]{1,0:T(8,128)(2,1)} %get-tuple-element.205), channel_id=1, source_target_pairs={{496,0},{0,16},{16,32},{32,48},{48,64},{64,80},{80,96},{96,112},{1... | collective-permute-start | bytes 589832 | tf_op jit(solution)/shard_map/while/body/eval_jaxpr/ppermute | solution.py:11
  388.1 9.3 %collective-permute-start = (bf16[48,2048]{1,0:T(8,128)(2,1)}, bf16[48,2048]{1,0:T(8,128)(2,1)S(1)}, u32[]{:S(2)}, u32[]{:S(2)}) collective-permute-start(bf16[48,2048]{1,0:T(8,128)(2,1)} %get-tuple-element.205), channel_id=1, source_target_pairs={{496,0},{0,16},{16,32},{32,48},{48,64},{64,80},{80,96},{96,112},{1... | collective-permute-start | bytes 589832 | tf_op jit(solution)/shard_map/while/body/eval_jaxpr/ppermute | solution.py:11
  399.7 9.3 %collective-permute-start = (bf16[48,2048]{1,0:T(8,128)(2,1)}, bf16[48,2048]{1,0:T(8,128)(2,1)S(1)}, u32[]{:S(2)}, u32[]{:S(2)}) collective-permute-start(bf16[48,2048]{1,0:T(8,128)(2,1)} %get-tuple-element.205), channel_id=1, source_target_pairs={{496,0},{0,16},{16,32},{32,48},{48,64},{64,80},{80,96},{96,112},{1... | collective-permute-start | bytes 589832 | tf_op jit(solution)/shard_map/while/body/eval_jaxpr/ppermute | solution.py:11
  411.4 9.3 %collective-permute-start = (bf16[48,2048]{1,0:T(8,128)(2,1)}, bf16[48,2048]{1,0:T(8,128)(2,1)S(1)}, u32[]{:S(2)}, u32[]{:S(2)}) collective-permute-start(bf16[48,2048]{1,0:T(8,128)(2,1)} %get-tuple-element.205), channel_id=1, source_target_pairs={{496,0},{0,16},{16,32},{32,48},{48,64},{64,80},{80,96},{96,112},{1... | collective-permute-start | bytes 589832 | tf_op jit(solution)/shard_map/while/body/eval_jaxpr/ppermute | solution.py:11
  423.1 9.3 %collective-permute-start = (bf16[48,2048]{1,0:T(8,128)(2,1)}, bf16[48,2048]{1,0:T(8,128)(2,1)S(1)}, u32[]{:S(2)}, u32[]{:S(2)}) collective-permute-start(bf16[48,2048]{1,0:T(8,128)(2,1)} %get-tuple-element.205), channel_id=1, source_target_pairs={{496,0},{0,16},{16,32},{32,48},{48,64},{64,80},{80,96},{96,112},{1... | collective-permute-start | bytes 589832 | tf_op jit(solution)/shard_map/while/body/eval_jaxpr/ppermute | solution.py:11
  434.7 9.3 %collective-permute-start = (bf16[48,2048]{1,0:T(8,128)(2,1)}, bf16[48,2048]{1,0:T(8,128)(2,1)S(1)}, u32[]{:S(2)}, u32[]{:S(2)}) collective-permute-start(bf16[48,2048]{1,0:T(8,128)(2,1)} %get-tuple-element.205), channel_id=1, source_target_pairs={{496,0},{0,16},{16,32},{32,48},{48,64},{64,80},{80,96},{96,112},{1... | collective-permute-start | bytes 589832 | tf_op jit(solution)/shard_map/while/body/eval_jaxpr/ppermute | solution.py:11
  446.4 9.3 %collective-permute-start = (bf16[48,2048]{1,0:T(8,128)(2,1)}, bf16[48,2048]{1,0:T(8,128)(2,1)S(1)}, u32[]{:S(2)}, u32[]{:S(2)}) collective-permute-start(bf16[48,2048]{1,0:T(8,128)(2,1)} %get-tuple-element.205), channel_id=1, source_target_pairs={{496,0},{0,16},{16,32},{32,48},{48,64},{64,80},{80,96},{96,112},{1... | collective-permute-start | bytes 589832 | tf_op jit(solution)/shard_map/while/body/eval_jaxpr/ppermute | solution.py:11
  458.1 9.3 %collective-permute-start = (bf16[48,2048]{1,0:T(8,128)(2,1)}, bf16[48,2048]{1,0:T(8,128)(2,1)S(1)}, u32[]{:S(2)}, u32[]{:S(2)}) collective-permute-start(bf16[48,2048]{1,0:T(8,128)(2,1)} %get-tuple-element.205), channel_id=1, source_target_pairs={{496,0},{0,16},{16,32},{32,48},{48,64},{64,80},{80,96},{96,112},{1... | collective-permute-start | bytes 589832 | tf_op jit(solution)/shard_map/while/body/eval_jaxpr/ppermute | solution.py:11
  493.1 9.3 %collective-permute-start = (bf16[48,2048]{1,0:T(8,128)(2,1)}, bf16[48,2048]{1,0:T(8,128)(2,1)S(1)}, u32[]{:S(2)}, u32[]{:S(2)}) collective-permute-start(bf16[48,2048]{1,0:T(8,128)(2,1)} %get-tuple-element.205), channel_id=1, source_target_pairs={{496,0},{0,16},{16,32},{32,48},{48,64},{64,80},{80,96},{96,112},{1... | collective-permute-start | bytes 589832 | tf_op jit(solution)/shard_map/while/body/eval_jaxpr/ppermute | solution.py:11
  (12 other events, 215.2 us)
where the time goes:
time: 518 us; the launch traced here: 516 us
  waiting for transfers between devices  228 us (44%)
  blocking collectives  95.6 us (18%)
  matrix products  74.3 us (14%)
  starting transfers between devices  67.7 us (13%)
  local copies, waits for them, and re-layouts  44.1 us (9%)
  other arithmetic  5.48 us (1%)
    ppermute x31, waiting for transfers between devices, from_behind(): return lax.ppermute(block, axis, route)  228 us
    all_gather x1, blocking collectives, body(): local_queries = lax.all_gather(queries, 'prod', axis=0, tiled=True)  95.6 us
    ppermute x31, starting transfers between devices, from_behind(): return lax.ppermute(block, axis, route)  59.1 us
    dot_general x32, matrix products, fill_tile(): lax.dot_general(local_block, stored, (((1,), (1,)), ((), ())), preferred_...  55.2 us
    while x31, local copies, waits for them, and re-layouts  20.9 us
  transfers between devices with their start and end apart: 32, of which 31 were waited for; matrix products, arithmetic and copies ran while one was open for 0% of the time, Pallas kernels for 0%

commit v1 on v0

--- a/solution.py
+++ b/solution.py
@@ -45,7 +45,9 @@
     bucket = 2 * row_count // owners
     capacity = owners * bucket
     places = destinations * bucket + row_ranks(destinations, owners)
-    local_queries = lax.all_gather(queries, "prod", axis=0, tiled=True)
+    local_queries = jnp.concatenate(
+        lax.all_to_all(jnp.stack([queries] * lax.axis_size("prod")), "prod", 0, 0), axis=0
+    )
     blank_scores = jnp.zeros((local_queries.shape[0] * owners, capacity), jnp.bfloat16)
     buffer = jnp.zeros((capacity, feature_width), jnp.bfloat16).at[places].set(gradients)
     buffer = buffer.reshape((owners, bucket, feature_width))

time: 518 us -> 524 us (1.012)
  the two profiles are of different devices: /device:TPU:258 before, /device:TPU:16 now
where the time goes in v1:
time: 524 us; the launch traced here: 523 us
  waiting for transfers between devices  312 us (60%)
  starting transfers between devices  79.8 us (15%)
  matrix products  74.3 us (14%)
  local copies, waits for them, and re-layouts  49 us (9%)
  other arithmetic  6.44 us (1%)
    ppermute x31, waiting for transfers between devices, from_behind(): return lax.ppermute(block, axis, route)  228 us
    all_to_all x1, waiting for transfers between devices, body(): lax.all_to_all(buffer, 'store', split_axis=0, concat_axis=0, tiled=True)  82 us
    ppermute x31, starting transfers between devices, from_behind(): return lax.ppermute(block, axis, route)  59.1 us
    dot_general x32, matrix products, fill_tile(): lax.dot_general(local_block, stored, (((1,), (1,)), ((), ())), preferred_...  55.2 us
    while x31, local copies, waits for them, and re-layouts  20.9 us
    all_to_all x1, starting transfers between devices, body(): lax.all_to_all(buffer, 'store', split_axis=0, concat_axis=0, tiled=True)  10.7 us
  transfers between devices with their start and end apart: 33, of which 33 were waited for; matrix products, arithmetic and copies ran while one was open for 2% of the time, Pallas kernels for 0%

profile of v1, /device:TPU:16, one launch (start us, length us, event | category | flops | bytes accessed | tf_op | source)
XLA Modules:
  0.0 523.1 jit_solution(13592031051531053660)
XLA Ops:
  1.5 9.9 %all-to-all-start.1 = ((bf16[16,3,2048]{2,1,0:T(4,128)(2,1)}), bf16[16,3,2048]{2,1,0:T(4,128)(2,1)S(1)}, u32[]{:S(2)}, u32[]{:S(2)}) async-start(bf16[16,3,2048]{2,1,0:T(4,128)(2,1)} %stack.2), calls=%async_computation.1 | async-start | bytes 524288 | tf_op jit(solution)/shard_map/all_to_all | solution.py:49
  22.9 10.7 %all-to-all-start = ((bf16[32,24,2048]{2,1,0:T(8,128)(2,1)}), bf16[32,24,2048]{2,1,0:T(8,128)(2,1)S(1)}, u32[]{:S(2)}, u32[]{:S(2)}) async-start(bf16[32,24,2048]{2,1,0:T(8,128)(2,1)} %bitcast.2), calls=%async_computation | async-start | bytes 6291456 | tf_op jit(solution)/shard_map/all_to_all | solution.py:55
  34.5 82.0 %all-to-all-done = bf16[32,24,2048]{2,1,0:T(8,128)(2,1)S(1)} async-done(((bf16[32,24,2048]{2,1,0:T(8,128)(2,1)}), bf16[32,24,2048]{2,1,0:T(8,128)(2,1)S(1)}, u32[]{:S(2)}, u32[]{:S(2)}) %all-to-all-start) | async-done | bytes 3145760 | tf_op jit(solution)/shard_map/all_to_all | solution.py:55
  116.5 7.6 %reshape.53 = bf16[768,32,64]{2,1,0:T(8,128)(2,1)} reshape(bf16[32,24,2048]{2,1,0:T(8,128)(2,1)S(1)} %all-to-all-done) | data formatting | bytes 6291456 | tf_op jit(solution)/shard_map/reshape | solution.py:18
  124.1 9.0 %fusion.5 = f32[768,32,64]{0,2,1:T(8,128)S(1)} fusion(bf16[768,32,64]{2,1,0:T(8,128)(2,1)} %reshape.53, f32[64,64]{1,0:T(8,128)S(1)} %copy-done), kind=kOutput, calls=%fused_computation.8 | convolution fusion | flops 1207959552 | bytes 9453568 | tf_op jit(solution)/shard_map/nbc,cd->nbd/dot_general | solution.py:19
  133.2 10.1 %multiply_reduce_fusion = (f32[768]{0:T(1024)S(1)}, f32[768,32,64]{0,1,2:T(8,128)S(1)}) fusion(f32[32,32]{1,0:T(8,128)S(1)} %copy-done.2, f32[768,32,64]{0,2,1:T(8,128)S(1)} %fusion.5), kind=kOutput, calls=%fused_computation.11 | convolution fusion | flops 607124736 | bytes 12590080 | tf_op jit(solution)/shard_map/ab,nbd->nad/dot_general | solution.py:20
  161.4 361.7 %while.17 = (s32[]{:T(128)}, bf16[1536,768]{1,0:T(8,128)(2,1)}, bf16[48,2048]{1,0:T(8,128)(2,1)}, bf16[768,2048]{1,0:T(8,128)(2,1)S(1)}, s32[]{:T(128)}, /*index...) while((s32[]{:T(128)}, bf16[1536,768]{1,0:T(8,128)(2,1)}, ...), condition=%wide.region_6.7_spmd, body=%wide.region_5.6_spmd.sunk | while | flops 151031824 | bytes 4596032 | solution.py:67
  163.3 7.4 %collective-permute-done = bf16[48,2048]{1,0:T(8,128)(2,1)S(1)} collective-permute-done((bf16[48,2048]{1,0:T(8,128)(2,1)}, bf16[48,2048]{1,0:T(8,128)(2,1)S(1)}, u32[]{:S(2)}, u32[]{:S(2)}) %collective-permute-start) | collective-permute-done | bytes 196640 | tf_op jit(solution)/shard_map/while/body/eval_jaxpr/ppermute | solution.py:11
  175.0 7.4 %collective-permute-done = bf16[48,2048]{1,0:T(8,128)(2,1)S(1)} collective-permute-done((bf16[48,2048]{1,0:T(8,128)(2,1)}, bf16[48,2048]{1,0:T(8,128)(2,1)S(1)}, u32[]{:S(2)}, u32[]{:S(2)}) %collective-permute-start) | collective-permute-done | bytes 196640 | tf_op jit(solution)/shard_map/while/body/eval_jaxpr/ppermute | solution.py:11
  186.7 7.4 %collective-permute-done = bf16[48,2048]{1,0:T(8,128)(2,1)S(1)} collective-permute-done((bf16[48,2048]{1,0:T(8,128)(2,1)}, bf16[48,2048]{1,0:T(8,128)(2,1)S(1)}, u32[]{:S(2)}, u32[]{:S(2)}) %collective-permute-start) | collective-permute-done | bytes 196640 | tf_op jit(solution)/shard_map/while/body/eval_jaxpr/ppermute | solution.py:11
  198.3 7.4 %collective-permute-done = bf16[48,2048]{1,0:T(8,128)(2,1)S(1)} collective-permute-done((bf16[48,2048]{1,0:T(8,128)(2,1)}, bf16[48,2048]{1,0:T(8,128)(2,1)S(1)}, u32[]{:S(2)}, u32[]{:S(2)}) %collective-permute-start) | collective-permute-done | bytes 196640 | tf_op jit(solution)/shard_map/while/body/eval_jaxpr/ppermute | solution.py:11
  210.0 7.4 %collective-permute-done = bf16[48,2048]{1,0:T(8,128)(2,1)S(1)} collective-permute-done((bf16[48,2048]{1,0:T(8,128)(2,1)}, bf16[48,2048]{1,0:T(8,128)(2,1)S(1)}, u32[]{:S(2)}, u32[]{:S(2)}) %collective-permute-start) | collective-permute-done | bytes 196640 | tf_op jit(solution)/shard_map/while/body/eval_jaxpr/ppermute | solution.py:11
  221.7 7.4 %collective-permute-done = bf16[48,2048]{1,0:T(8,128)(2,1)S(1)} collective-permute-done((bf16[48,2048]{1,0:T(8,128)(2,1)}, bf16[48,2048]{1,0:T(8,128)(2,1)S(1)}, u32[]{:S(2)}, u32[]{:S(2)}) %collective-permute-start) | collective-permute-done | bytes 196640 | tf_op jit(solution)/shard_map/while/body/eval_jaxpr/ppermute | solution.py:11
  233.3 7.4 %collective-permute-done = bf16[48,2048]{1,0:T(8,128)(2,1)S(1)} collective-permute-done((bf16[48,2048]{1,0:T(8,128)(2,1)}, bf16[48,2048]{1,0:T(8,128)(2,1)S(1)}, u32[]{:S(2)}, u32[]{:S(2)}) %collective-permute-start) | collective-permute-done | bytes 196640 | tf_op jit(solution)/shard_map/while/body/eval_jaxpr/ppermute | solution.py:11
  256.7 7.4 %collective-permute-done = bf16[48,2048]{1,0:T(8,128)(2,1)S(1)} collective-permute-done((bf16[48,2048]{1,0:T(8,128)(2,1)}, bf16[48,2048]{1,0:T(8,128)(2,1)S(1)}, u32[]{:S(2)}, u32[]{:S(2)}) %collective-permute-start) | collective-permute-done | bytes 196640 | tf_op jit(solution)/shard_map/while/body/eval_jaxpr/ppermute | solution.py:11
  291.7 7.4 %collective-permute-done = bf16[48,2048]{1,0:T(8,128)(2,1)S(1)} collective-permute-done((bf16[48,2048]{1,0:T(8,128)(2,1)}, bf16[48,2048]{1,0:T(8,128)(2,1)S(1)}, u32[]{:S(2)}, u32[]{:S(2)}) %collective-permute-start) | collective-permute-done | bytes 196640 | tf_op jit(solution)/shard_map/while/body/eval_jaxpr/ppermute | solution.py:11
  303.3 7.4 %collective-permute-done = bf16[48,2048]{1,0:T(8,128)(2,1)S(1)} collective-permute-done((bf16[48,2048]{1,0:T(8,128)(2,1)}, bf16[48,2048]{1,0:T(8,128)(2,1)S(1)}, u32[]{:S(2)}, u32[]{:S(2)}) %collective-permute-start) | collective-permute-done | bytes 196640 | tf_op jit(solution)/shard_map/while/body/eval_jaxpr/ppermute | solution.py:11
  315.0 7.4 %collective-permute-done = bf16[48,2048]{1,0:T(8,128)(2,1)S(1)} collective-permute-done((bf16[48,2048]{1,0:T(8,128)(2,1)}, bf16[48,2048]{1,0:T(8,128)(2,1)S(1)}, u32[]{:S(2)}, u32[]{:S(2)}) %collective-permute-start) | collective-permute-done | bytes 196640 | tf_op jit(solution)/shard_map/while/body/eval_jaxpr/ppermute | solution.py:11
  326.7 7.4 %collective-permute-done = bf16[48,2048]{1,0:T(8,128)(2,1)S(1)} collective-permute-done((bf16[48,2048]{1,0:T(8,128)(2,1)}, bf16[48,2048]{1,0:T(8,128)(2,1)S(1)}, u32[]{:S(2)}, u32[]{:S(2)}) %collective-permute-start) | collective-permute-done | bytes 196640 | tf_op jit(solution)/shard_map/while/body/eval_jaxpr/ppermute | solution.py:11
  338.3 7.4 %collective-permute-done = bf16[48,2048]{1,0:T(8,128)(2,1)S(1)} collective-permute-done((bf16[48,2048]{1,0:T(8,128)(2,1)}, bf16[48,2048]{1,0:T(8,128)(2,1)S(1)}, u32[]{:S(2)}, u32[]{:S(2)}) %collective-permute-start) | collective-permute-done | bytes 196640 | tf_op jit(solution)/shard_map/while/body/eval_jaxpr/ppermute | solution.py:11
  350.0 7.4 %collective-permute-done = bf16[48,2048]{1,0:T(8,128)(2,1)S(1)} collective-permute-done((bf16[48,2048]{1,0:T(8,128)(2,1)}, bf16[48,2048]{1,0:T(8,128)(2,1)S(1)}, u32[]{:S(2)}, u32[]{:S(2)}) %collective-permute-start) | collective-permute-done | bytes 196640 | tf_op jit(solution)/shard_map/while/body/eval_jaxpr/ppermute | solution.py:11
  361.7 7.4 %collective-permute-done = bf16[48,2048]{1,0:T(8,128)(2,1)S(1)} collective-permute-done((bf16[48,2048]{1,0:T(8,128)(2,1)}, bf16[48,2048]{1,0:T(8,128)(2,1)S(1)}, u32[]{:S(2)}, u32[]{:S(2)}) %collective-permute-start) | collective-permute-done | bytes 196640 | tf_op jit(solution)/shard_map/while/body/eval_jaxpr/ppermute | solution.py:11
  373.3 7.4 %collective-permute-done = bf16[48,2048]{1,0:T(8,128)(2,1)S(1)} collective-permute-done((bf16[48,2048]{1,0:T(8,128)(2,1)}, bf16[48,2048]{1,0:T(8,128)(2,1)S(1)}, u32[]{:S(2)}, u32[]{:S(2)}) %collective-permute-start) | collective-permute-done | bytes 196640 | tf_op jit(solution)/shard_map/while/body/eval_jaxpr/ppermute | solution.py:11
  385.0 7.4 %collective-permute-done = bf16[48,2048]{1,0:T(8,128)(2,1)S(1)} collective-permute-done((bf16[48,2048]{1,0:T(8,128)(2,1)}, bf16[48,2048]{1,0:T(8,128)(2,1)S(1)}, u32[]{:S(2)}, u32[]{:S(2)}) %collective-permute-start) | collective-permute-done | bytes 196640 | tf_op jit(solution)/shard_map/while/body/eval_jaxpr/ppermute | solution.py:11
  (131 shorter events, 267.4 us)
Async XLA Ops:
  1.5 21.4 %all-to-all-start.1 = ((bf16[16,3,2048]{2,1,0:T(4,128)(2,1)}), bf16[16,3,2048]{2,1,0:T(4,128)(2,1)S(1)}, u32[]{:S(2)}, u32[]{:S(2)}) async-start(bf16[16,3,2048]{2,1,0:T(4,128)(2,1)} %stack.2), calls=%async_computation.1 | async-start | bytes 524288 | tf_op jit(solution)/shard_map/all_to_all | solution.py:49
  22.9 93.6 %all-to-all-start = ((bf16[32,24,2048]{2,1,0:T(8,128)(2,1)}), bf16[32,24,2048]{2,1,0:T(8,128)(2,1)S(1)}, u32[]{:S(2)}, u32[]{:S(2)}) async-start(bf16[32,24,2048]{2,1,0:T(8,128)(2,1)} %bitcast.2), calls=%async_computation | async-start | bytes 6291456 | tf_op jit(solution)/shard_map/all_to_all | solution.py:55
  173.1 9.3 %collective-permute-start = (bf16[48,2048]{1,0:T(8,128)(2,1)}, bf16[48,2048]{1,0:T(8,128)(2,1)S(1)}, u32[]{:S(2)}, u32[]{:S(2)}) collective-permute-start(bf16[48,2048]{1,0:T(8,128)(2,1)} %get-tuple-element.200), channel_id=1, source_target_pairs={{496,0},{0,16},{16,32},{32,48},{48,64},{64,80},{80,96},{96,112},{1... | collective-permute-start | bytes 589832 | tf_op jit(solution)/shard_map/while/body/eval_jaxpr/ppermute | solution.py:11
  184.7 9.3 %collective-permute-start = (bf16[48,2048]{1,0:T(8,128)(2,1)}, bf16[48,2048]{1,0:T(8,128)(2,1)S(1)}, u32[]{:S(2)}, u32[]{:S(2)}) collective-permute-start(bf16[48,2048]{1,0:T(8,128)(2,1)} %get-tuple-element.200), channel_id=1, source_target_pairs={{496,0},{0,16},{16,32},{32,48},{48,64},{64,80},{80,96},{96,112},{1... | collective-permute-start | bytes 589832 | tf_op jit(solution)/shard_map/while/body/eval_jaxpr/ppermute | solution.py:11
  196.4 9.3 %collective-permute-start = (bf16[48,2048]{1,0:T(8,128)(2,1)}, bf16[48,2048]{1,0:T(8,128)(2,1)S(1)}, u32[]{:S(2)}, u32[]{:S(2)}) collective-permute-start(bf16[48,2048]{1,0:T(8,128)(2,1)} %get-tuple-element.200), channel_id=1, source_target_pairs={{496,0},{0,16},{16,32},{32,48},{48,64},{64,80},{80,96},{96,112},{1... | collective-permute-start | bytes 589832 | tf_op jit(solution)/shard_map/while/body/eval_jaxpr/ppermute | solution.py:11
  208.1 9.3 %collective-permute-start = (bf16[48,2048]{1,0:T(8,128)(2,1)}, bf16[48,2048]{1,0:T(8,128)(2,1)S(1)}, u32[]{:S(2)}, u32[]{:S(2)}) collective-permute-start(bf16[48,2048]{1,0:T(8,128)(2,1)} %get-tuple-element.200), channel_id=1, source_target_pairs={{496,0},{0,16},{16,32},{32,48},{48,64},{64,80},{80,96},{96,112},{1... | collective-permute-start | bytes 589832 | tf_op jit(solution)/shard_map/while/body/eval_jaxpr/ppermute | solution.py:11
  219.7 9.3 %collective-permute-start = (bf16[48,2048]{1,0:T(8,128)(2,1)}, bf16[48,2048]{1,0:T(8,128)(2,1)S(1)}, u32[]{:S(2)}, u32[]{:S(2)}) collective-permute-start(bf16[48,2048]{1,0:T(8,128)(2,1)} %get-tuple-element.200), channel_id=1, source_target_pairs={{496,0},{0,16},{16,32},{32,48},{48,64},{64,80},{80,96},{96,112},{1... | collective-permute-start | bytes 589832 | tf_op jit(solution)/shard_map/while/body/eval_jaxpr/ppermute | solution.py:11
  231.4 9.3 %collective-permute-start = (bf16[48,2048]{1,0:T(8,128)(2,1)}, bf16[48,2048]{1,0:T(8,128)(2,1)S(1)}, u32[]{:S(2)}, u32[]{:S(2)}) collective-permute-start(bf16[48,2048]{1,0:T(8,128)(2,1)} %get-tuple-element.200), channel_id=1, source_target_pairs={{496,0},{0,16},{16,32},{32,48},{48,64},{64,80},{80,96},{96,112},{1... | collective-permute-start | bytes 589832 | tf_op jit(solution)/shard_map/while/body/eval_jaxpr/ppermute | solution.py:11
  254.7 9.3 %collective-permute-start = (bf16[48,2048]{1,0:T(8,128)(2,1)}, bf16[48,2048]{1,0:T(8,128)(2,1)S(1)}, u32[]{:S(2)}, u32[]{:S(2)}) collective-permute-start(bf16[48,2048]{1,0:T(8,128)(2,1)} %get-tuple-element.200), channel_id=1, source_target_pairs={{496,0},{0,16},{16,32},{32,48},{48,64},{64,80},{80,96},{96,112},{1... | collective-permute-start | bytes 589832 | tf_op jit(solution)/shard_map/while/body/eval_jaxpr/ppermute | solution.py:11
  289.7 9.3 %collective-permute-start = (bf16[48,2048]{1,0:T(8,128)(2,1)}, bf16[48,2048]{1,0:T(8,128)(2,1)S(1)}, u32[]{:S(2)}, u32[]{:S(2)}) collective-permute-start(bf16[48,2048]{1,0:T(8,128)(2,1)} %get-tuple-element.200), channel_id=1, source_target_pairs={{496,0},{0,16},{16,32},{32,48},{48,64},{64,80},{80,96},{96,112},{1... | collective-permute-start | bytes 589832 | tf_op jit(solution)/shard_map/while/body/eval_jaxpr/ppermute | solution.py:11
  301.4 9.3 %collective-permute-start = (bf16[48,2048]{1,0:T(8,128)(2,1)}, bf16[48,2048]{1,0:T(8,128)(2,1)S(1)}, u32[]{:S(2)}, u32[]{:S(2)}) collective-permute-start(bf16[48,2048]{1,0:T(8,128)(2,1)} %get-tuple-element.200), channel_id=1, source_target_pairs={{496,0},{0,16},{16,32},{32,48},{48,64},{64,80},{80,96},{96,112},{1... | collective-permute-start | bytes 589832 | tf_op jit(solution)/shard_map/while/body/eval_jaxpr/ppermute | solution.py:11
  313.1 9.3 %collective-permute-start = (bf16[48,2048]{1,0:T(8,128)(2,1)}, bf16[48,2048]{1,0:T(8,128)(2,1)S(1)}, u32[]{:S(2)}, u32[]{:S(2)}) collective-permute-start(bf16[48,2048]{1,0:T(8,128)(2,1)} %get-tuple-element.200), channel_id=1, source_target_pairs={{496,0},{0,16},{16,32},{32,48},{48,64},{64,80},{80,96},{96,112},{1... | collective-permute-start | bytes 589832 | tf_op jit(solution)/shard_map/while/body/eval_jaxpr/ppermute | solution.py:11
  324.7 9.3 %collective-permute-start = (bf16[48,2048]{1,0:T(8,128)(2,1)}, bf16[48,2048]{1,0:T(8,128)(2,1)S(1)}, u32[]{:S(2)}, u32[]{:S(2)}) collective-permute-start(bf16[48,2048]{1,0:T(8,128)(2,1)} %get-tuple-element.200), channel_id=1, source_target_pairs={{496,0},{0,16},{16,32},{32,48},{48,64},{64,80},{80,96},{96,112},{1... | collective-permute-start | bytes 589832 | tf_op jit(solution)/shard_map/while/body/eval_jaxpr/ppermute | solution.py:11
  336.4 9.3 %collective-permute-start = (bf16[48,2048]{1,0:T(8,128)(2,1)}, bf16[48,2048]{1,0:T(8,128)(2,1)S(1)}, u32[]{:S(2)}, u32[]{:S(2)}) collective-permute-start(bf16[48,2048]{1,0:T(8,128)(2,1)} %get-tuple-element.200), channel_id=1, source_target_pairs={{496,0},{0,16},{16,32},{32,48},{48,64},{64,80},{80,96},{96,112},{1... | collective-permute-start | bytes 589832 | tf_op jit(solution)/shard_map/while/body/eval_jaxpr/ppermute | solution.py:11
  348.1 9.3 %collective-permute-start = (bf16[48,2048]{1,0:T(8,128)(2,1)}, bf16[48,2048]{1,0:T(8,128)(2,1)S(1)}, u32[]{:S(2)}, u32[]{:S(2)}) collective-permute-start(bf16[48,2048]{1,0:T(8,128)(2,1)} %get-tuple-element.200), channel_id=1, source_target_pairs={{496,0},{0,16},{16,32},{32,48},{48,64},{64,80},{80,96},{96,112},{1... | collective-permute-start | bytes 589832 | tf_op jit(solution)/shard_map/while/body/eval_jaxpr/ppermute | solution.py:11
  359.7 9.3 %collective-permute-start = (bf16[48,2048]{1,0:T(8,128)(2,1)}, bf16[48,2048]{1,0:T(8,128)(2,1)S(1)}, u32[]{:S(2)}, u32[]{:S(2)}) collective-permute-start(bf16[48,2048]{1,0:T(8,128)(2,1)} %get-tuple-element.200), channel_id=1, source_target_pairs={{496,0},{0,16},{16,32},{32,48},{48,64},{64,80},{80,96},{96,112},{1... | collective-permute-start | bytes 589832 | tf_op jit(solution)/shard_map/while/body/eval_jaxpr/ppermute | solution.py:11
  371.4 9.3 %collective-permute-start = (bf16[48,2048]{1,0:T(8,128)(2,1)}, bf16[48,2048]{1,0:T(8,128)(2,1)S(1)}, u32[]{:S(2)}, u32[]{:S(2)}) collective-permute-start(bf16[48,2048]{1,0:T(8,128)(2,1)} %get-tuple-element.200), channel_id=1, source_target_pairs={{496,0},{0,16},{16,32},{32,48},{48,64},{64,80},{80,96},{96,112},{1... | collective-permute-start | bytes 589832 | tf_op jit(solution)/shard_map/while/body/eval_jaxpr/ppermute | solution.py:11
  383.1 9.3 %collective-permute-start = (bf16[48,2048]{1,0:T(8,128)(2,1)}, bf16[48,2048]{1,0:T(8,128)(2,1)S(1)}, u32[]{:S(2)}, u32[]{:S(2)}) collective-permute-start(bf16[48,2048]{1,0:T(8,128)(2,1)} %get-tuple-element.200), channel_id=1, source_target_pairs={{496,0},{0,16},{16,32},{32,48},{48,64},{64,80},{80,96},{96,112},{1... | collective-permute-start | bytes 589832 | tf_op jit(solution)/shard_map/while/body/eval_jaxpr/ppermute | solution.py:11
  394.7 9.3 %collective-permute-start = (bf16[48,2048]{1,0:T(8,128)(2,1)}, bf16[48,2048]{1,0:T(8,128)(2,1)S(1)}, u32[]{:S(2)}, u32[]{:S(2)}) collective-permute-start(bf16[48,2048]{1,0:T(8,128)(2,1)} %get-tuple-element.200), channel_id=1, source_target_pairs={{496,0},{0,16},{16,32},{32,48},{48,64},{64,80},{80,96},{96,112},{1... | collective-permute-start | bytes 589832 | tf_op jit(solution)/shard_map/while/body/eval_jaxpr/ppermute | solution.py:11
  418.1 9.3 %collective-permute-start = (bf16[48,2048]{1,0:T(8,128)(2,1)}, bf16[48,2048]{1,0:T(8,128)(2,1)S(1)}, u32[]{:S(2)}, u32[]{:S(2)}) collective-permute-start(bf16[48,2048]{1,0:T(8,128)(2,1)} %get-tuple-element.200), channel_id=1, source_target_pairs={{496,0},{0,16},{16,32},{32,48},{48,64},{64,80},{80,96},{96,112},{1... | collective-permute-start | bytes 589832 | tf_op jit(solution)/shard_map/while/body/eval_jaxpr/ppermute | solution.py:11
  441.4 9.3 %collective-permute-start = (bf16[48,2048]{1,0:T(8,128)(2,1)}, bf16[48,2048]{1,0:T(8,128)(2,1)S(1)}, u32[]{:S(2)}, u32[]{:S(2)}) collective-permute-start(bf16[48,2048]{1,0:T(8,128)(2,1)} %get-tuple-element.200), channel_id=1, source_target_pairs={{496,0},{0,16},{16,32},{32,48},{48,64},{64,80},{80,96},{96,112},{1... | collective-permute-start | bytes 589832 | tf_op jit(solution)/shard_map/while/body/eval_jaxpr/ppermute | solution.py:11
  453.1 9.3 %collective-permute-start = (bf16[48,2048]{1,0:T(8,128)(2,1)}, bf16[48,2048]{1,0:T(8,128)(2,1)S(1)}, u32[]{:S(2)}, u32[]{:S(2)}) collective-permute-start(bf16[48,2048]{1,0:T(8,128)(2,1)} %get-tuple-element.200), channel_id=1, source_target_pairs={{496,0},{0,16},{16,32},{32,48},{48,64},{64,80},{80,96},{96,112},{1... | collective-permute-start | bytes 589832 | tf_op jit(solution)/shard_map/while/body/eval_jaxpr/ppermute | solution.py:11
  464.7 9.3 %collective-permute-start = (bf16[48,2048]{1,0:T(8,128)(2,1)}, bf16[48,2048]{1,0:T(8,128)(2,1)S(1)}, u32[]{:S(2)}, u32[]{:S(2)}) collective-permute-start(bf16[48,2048]{1,0:T(8,128)(2,1)} %get-tuple-element.200), channel_id=1, source_target_pairs={{496,0},{0,16},{16,32},{32,48},{48,64},{64,80},{80,96},{96,112},{1... | collective-permute-start | bytes 589832 | tf_op jit(solution)/shard_map/while/body/eval_jaxpr/ppermute | solution.py:11
  476.4 9.3 %collective-permute-start = (bf16[48,2048]{1,0:T(8,128)(2,1)}, bf16[48,2048]{1,0:T(8,128)(2,1)S(1)}, u32[]{:S(2)}, u32[]{:S(2)}) collective-permute-start(bf16[48,2048]{1,0:T(8,128)(2,1)} %get-tuple-element.200), channel_id=1, source_target_pairs={{496,0},{0,16},{16,32},{32,48},{48,64},{64,80},{80,96},{96,112},{1... | collective-permute-start | bytes 589832 | tf_op jit(solution)/shard_map/while/body/eval_jaxpr/ppermute | solution.py:11
  (12 other events, 218.2 us)
